TPU v7x, 32 devices: a whole 2x2x4 slice. The times are simulated.
32 devices in a mesh: ent: 8 (over z, y), rep: 4 (over x, core).
Axes of the slice: x: 2, y: 2, z: 4, core: 2. Of those that a mesh axis runs over, the one named last changes fastest.
Arguments:
- table: float32 [32768, 256], P('ent'), may hold values from -6.1 to 6.1
- relations: float32 [824, 256], P('rep'), may hold values from -4 to 4
- anchor: int32 [2048], P('rep'), may hold values from 0 to 32767
- rel_one: int32 [2048], P('rep'), may hold values from 0 to 823
- rel_two: int32 [2048], P('rep'), may hold values from 0 to 823
Outputs:
- log_answer: float32 [2048, 32768], P('rep', 'ent')
All inputs are finite; a program needn't handle non-finite values.
Results may differ from a plain program's by a relative error of at most 0.00018.
Values sent between devices are 32-bit elements; how exact they have to be, the bound alone decides.
A program may use at most 128 MiB of HBM per device.

v0:
```python
import jax
import jax.numpy as jnp
from jax import lax
from jax.sharding import PartitionSpec as P


def cmul(left, right):
    half = left.shape[1] // 2
    lre, lim = (left[:, :half], left[:, half:])
    rre, rim = (right[:, :half], right[:, half:])
    return jnp.concatenate([lre * rre - lim * rim, lre * rim + lim * rre], axis=1)


def against(query, table):
    return lax.dot_general(
        query,
        table,
        (((1,), (1,)), ((), ())),
        precision=lax.Precision.HIGHEST,
        preferred_element_type=jnp.float32,
    )


def weighted(weights, table):
    return jnp.dot(
        weights, table, precision=lax.Precision.HIGHEST, preferred_element_type=jnp.float32
    )


def on_device(table, relations, anchor, rel_one, rel_two):
    rows = table.shape[0]
    start = lax.axis_index("ent") * rows
    offset = anchor - start
    inside = ((offset >= 0) & (offset < rows)).astype(jnp.float32)
    local_rows = jnp.take(table, jnp.clip(offset, 0, rows - 1), axis=0)
    anchor_emb = lax.psum(local_rows * inside[:, None], "ent")
    rel_all = lax.all_gather(relations, "rep", axis=0, tiled=True)
    rel_first = jnp.take(rel_all, rel_one, axis=0)
    rel_second = jnp.take(rel_all, rel_two, axis=0)
    query_one = cmul(anchor_emb, rel_first)
    scores = against(query_one, table)
    local_peak = jnp.max(scores, axis=1)
    peak = lax.pmax(local_peak, "ent")
    weights = jnp.exp(scores - peak[:, None])
    total, summed = lax.psum((jnp.sum(weights, axis=1), weighted(weights, table)), "ent")
    query_two = cmul(summed / total[:, None], rel_second)
    scores_two = against(query_two, table)
    local_top = jnp.max(scores_two, axis=1)
    top = lax.pmax(local_top, "ent")
    shifted = scores_two - top[:, None]
    mass = lax.psum(jnp.sum(jnp.exp(shifted), axis=1), "ent")
    return shifted - jnp.log(mass)[:, None]


def solution(mesh):
    in_specs = (P("ent", None), P("rep", None), P("rep"), P("rep"), P("rep"))
    out_specs = P("rep", "ent")
    return jax.shard_map(
        on_device, mesh=mesh, in_specs=in_specs, out_specs=out_specs, check_vma=False
    )
```

profile of v0, /device:TPU:0, one launch (start us, length us, event | category | flops | bytes accessed | tf_op | source)
XLA Modules:
  0.0 268.9 jit_solution(11767141147475864850)
XLA Ops:
  6.5 0.0 all-reduce.3.cloned.1.call-start
  6.5 0.7 compare_and_fusion.2
  7.2 0.0 copy-start
  7.2 3.8 %gather_fusion = f32[512,256]{1,0:T(8,128)S(1)} fusion(f32[4096,256]{1,0:T(8,128)} %param.7, s32[1024]{0:T(1024)S(1)} %pad_clamp_fusion.2), kind=kCustom, calls=%fused_computation.2 | custom fusion | bytes 1050624 | tf_op jit(solution)/shard_map/jit(_take)/gather | solution.py:35
  11.0 1.0 select_multiply_fusion
  12.0 0.0 all-reduce.3.cloned.1.call-update
  12.0 0.0 all-reduce.5.cloned.1.call-start
  12.1 0.7 compare_and_fusion.1
  12.8 0.7 compare_select_fusion.1
  13.5 0.7 compare_select_fusion
  14.2 10.6 %all-gather = f32[4,206,256]{2,1,0:T(8,128)S(1)} all-gather(f32[1,206,256]{2,1,0:T(8,128)} %bitcast.4), channel_id=1, replica_groups=mesh['ent'=8,'rep'=4] {'rep'}, dimensions={0}, use_global_device_ids=true | all-gather | bytes 1054720 | tf_op jit(solution)/shard_map/all_gather | solution.py:37
  24.8 0.1 reshape.43
  24.9 1.6 gather_fusion.2
  26.4 1.6 gather_fusion.1
  28.0 0.0 copy-done
  28.0 0.1 broadcast_select_fusion.1
  28.2 59.0 %all-reduce.3.cloned.1.call-done = f32[512,256]{1,0:T(8,128)} async-done(((f32[512,256]{1,0:T(8,128)}), f32[512,256]{1,0:T(8,128)}) %all-reduce.3.cloned.1.call-update) | async-done | bytes 524304 | tf_op jit(solution)/shard_map/psum | solution.py:36
  87.2 1.1 multiply_subtract_fusion.1
  88.3 10.9 %fusion.13 = (f32[512]{0:T(512)S(1)}, f32[512,4096]{1,0:T(8,128)}) fusion(f32[4096,256]{1,0:T(8,128)} %param.7, f32[512,128]{1,0:T(8,128)S(1)} %get-tuple-element.11, f32[512,128]{1,0:T(8,128)S(1)} %get-tuple-element.10), kind=kOutput, calls=%fused_computation.37 | convolution fusion | flops 6444678656 | bytes 13109248 | tf_op jit(solution)/shard_map/dot_general | solution.py:15
  99.2 19.7 %pmax.14 = f32[512]{0:T(512)S(1)} all-reduce(f32[512]{0:T(512)S(1)} %get-tuple-element.13), channel_id=1, replica_groups=mesh['ent'=8,'rep'=4] {'ent'}, use_global_device_ids=true, to_apply=%region_2.4 | all-reduce | flops 512 | bytes 4096 | tf_op jit(solution)/shard_map/pmax | solution.py:43
  118.9 11.2 %fusion.1 = f32[512,256]{1,0:T(8,128)} fusion(f32[4096,256]{1,0:T(8,128)} %param.7, f32[512,4096]{1,0:T(8,128)} %get-tuple-element.14, f32[512]{0:T(512)S(1)} %pmax.14), kind=kOutput, calls=%fused_computation.7 | convolution fusion | flops 6444548096 | bytes 13109248 | tf_op jit(solution)/shard_map/dot_general | solution.py:25
  130.1 0.0 all-reduce.5.cloned.1.call-update
  130.1 0.1 broadcast_select_fusion
  130.3 4.8 %fusion = f32[512]{0:T(512)S(1)} fusion(f32[512,4096]{1,0:T(8,128)} %get-tuple-element.14, f32[512]{0:T(512)S(1)} %pmax.14), kind=kLoop, calls=%fused_computation.6 | loop fusion | flops 4193792 | bytes 8392704 | tf_op jit(solution)/shard_map/reduce_sum | solution.py:45
  135.0 17.3 %psum.30 = f32[512]{0:T(512)S(1)} all-reduce(f32[512]{0:T(512)S(1)} %fusion), channel_id=1, replica_groups=mesh['ent'=8,'rep'=4] {'ent'}, use_global_device_ids=true, to_apply=%region_5.7 | all-reduce | flops 512 | bytes 4096 | tf_op jit(solution)/shard_map/psum | solution.py:45
  152.3 47.5 %all-reduce.5.cloned.1.call-done = f32[512,256]{1,0:T(8,128)} async-done(((f32[512,256]{1,0:T(8,128)}), f32[512,256]{1,0:T(8,128)}) %all-reduce.5.cloned.1.call-update) | async-done | bytes 524304 | tf_op jit(solution)/shard_map/psum | solution.py:45
  199.9 1.2 broadcast_divide_fusion
  201.1 0.1 multiply_subtract_fusion
  201.1 10.9 %fusion.14 = (f32[512]{0:T(512)S(1)}, f32[512,4096]{1,0:T(8,128)}) fusion(f32[4096,256]{1,0:T(8,128)} %param.7, f32[512,128]{1,0:T(8,128)S(1)} %get-tuple-element.9, f32[512,128]{1,0:T(8,128)S(1)} %get-tuple-element.8), kind=kOutput, calls=%fused_computation.38 | convolution fusion | flops 6444678656 | bytes 13109248 | tf_op jit(solution)/shard_map/dot_general | solution.py:15
  212.0 19.7 %pmax.15 = f32[512]{0:T(512)S(1)} all-reduce(f32[512]{0:T(512)S(1)} %get-tuple-element.15), channel_id=1, replica_groups=mesh['ent'=8,'rep'=4] {'ent'}, use_global_device_ids=true, to_apply=%region_7.9 | all-reduce | flops 512 | bytes 4096 | tf_op jit(solution)/shard_map/pmax | solution.py:49
  231.7 4.6 %exponential_reduce_fusion = f32[512]{0:T(512)S(1)} fusion(f32[512,4096]{1,0:T(8,128)} %get-tuple-element.16, f32[512]{0:T(512)S(1)} %pmax.15), kind=kLoop, calls=%fused_computation.3 | loop fusion | flops 4193792 | bytes 8392704 | tf_op jit(solution)/shard_map/reduce_sum | solution.py:51
  236.3 17.1 %psum.31 = f32[512]{0:T(512)S(1)} all-reduce(f32[512]{0:T(512)S(1)} %exponential_reduce_fusion), channel_id=1, replica_groups=mesh['ent'=8,'rep'=4] {'ent'}, use_global_device_ids=true, to_apply=%region_9.11 | all-reduce | flops 512 | bytes 4096 | tf_op jit(solution)/shard_map/psum | solution.py:51
  253.4 8.6 %subtract_subtract_fusion = f32[512,4096]{1,0:T(8,128)} fusion(f32[512,4096]{1,0:T(8,128)} %get-tuple-element.16, f32[512]{0:T(512)S(1)} %log.3, f32[512]{0:T(512)S(1)} %pmax.15), kind=kLoop, calls=%fused_computation.5 | loop fusion | flops 4194304 | bytes 16781312 | tf_op jit(solution)/shard_map/sub | solution.py:52
  (5 shorter events, 0.0 us)
Async XLA Ops:
  6.5 80.7 %all-reduce.3.cloned.1.call-start = ((), (), s32[]{:S(2)}) async-start(), calls=%async_computation | async-start | bytes 1048576 | tf_op jit(solution)/shard_map/psum | solution.py:36
  7.2 20.8 %copy-start = (s32[512]{0:T(512)S(1)}, s32[512]{0:T(512)}, u32[]{:S(2)}) copy-start(s32[512]{0:T(512)} %param.11) | copy-start | bytes 6148
  12.0 187.8 %all-reduce.5.cloned.1.call-start = ((), (), s32[]{:S(2)}) async-start(), calls=%async_computation.1 | async-start | bytes 1048576 | tf_op jit(solution)/shard_map/psum | solution.py:45
Sparse Core Ops, SparseCore 0:
  12.2 75.0 all-reduce.2
  130.2 69.5 all-reduce.4
where the time goes:
time: 269 us
  waiting for transfers between devices  107 us (40%)
  blocking collectives  84.4 us (31%)
  matrix products  33 us (12%)
  other arithmetic  24.3 us (9%)
  between operations  13.5 us (5%)
  local copies, waits for them, and re-layouts  7.02 us (3%)
    psum x1, waiting for transfers between devices, on_device(): anchor_emb = lax.psum(local_rows * inside[:, None], 'ent')  59 us
    psum x1, waiting for transfers between devices, on_device(): lax.psum((jnp.sum(weights, axis=1), weighted(weights, table)), 'ent')  47.5 us
    dot_general x2, matrix products, against(): lax.dot_general(query, table, (((1,), (1,)), ((), ())), precision=lax.Pre...  21.8 us
    pmax x1, blocking collectives, on_device(): peak = lax.pmax(local_peak, 'ent')  19.7 us
    pmax x1, blocking collectives, on_device(): top = lax.pmax(local_top, 'ent')  19.7 us
    psum x1, blocking collectives, on_device(): lax.psum((jnp.sum(weights, axis=1), weighted(weights, table)), 'ent')  17.3 us
    psum x1, blocking collectives, on_device(): mass = lax.psum(jnp.sum(jnp.exp(shifted), axis=1), 'ent')  17.1 us
    dot_general x1, matrix products, weighted(): jnp.dot(weights, table, precision=lax.Precision.HIGHEST, preferred_elemen...  11.2 us
  transfers between devices with their start and end apart: 2, of which 2 were waited for; matrix products, arithmetic and copies ran while one was open for 4% of the time, Pallas kernels for 0%

commit v1 on v0

v1 whole, which is shorter than its diff:
```python
import functools

import jax
import jax.numpy as jnp
from jax import lax
from jax.experimental import pallas as pl
from jax.experimental.pallas import tpu as pltpu
from jax.sharding import PartitionSpec as P

MESH = pl.DeviceIdType.MESH
F32, BF16 = jnp.float32, jnp.bfloat16


def cmul(left, right):
    half = left.shape[1] // 2
    lre, lim = left[:, :half], left[:, half:]
    rre, rim = right[:, :half], right[:, half:]
    return jnp.concatenate([lre * rre - lim * rim, lre * rim + lim * rre], axis=1)


def halves(x):
    high = x.astype(BF16)
    return high, (x - high.astype(F32)).astype(BF16)


def dot(a, b, contract):
    return lax.dot_general(a, b, (contract, ((), ())), preferred_element_type=F32)


def dot3(a, b, contract):
    return dot(a[0], b[0], contract) + (dot(a[0], b[1], contract) + dot(a[1], b[0], contract))


NT = ((1,), (1,))
NN = ((1,), (0,))


def kernel(
    n, m, tile, block,
    table, relations, anchor, rel_one, rel_two,
    scores_out, lse_out,
    t_hi, t_lo, scores, asend, arecv, rels, r1, r2, acc, q1, q2, csend, crecv, erecv, esend,
    sa, ra, sr, rr, sb, rb, sc, rc, sd, rd, se, re, so,
):
    me, mine = lax.axis_index("ent"), lax.axis_index("rep")
    rows, width = q1.shape
    chunk = rows // n
    ents = table.shape[0]
    start = me * ents
    nrel = relations.shape[0]

    def to(k):
        return lax.rem(me + k, n)

    def source(k):
        return lax.rem(me - k + n, n)

    def at(d):
        return pl.ds(pl.multiple_of(d * chunk, 8), chunk)

    def ent_copy(src, dst, send, recv, k):
        return pltpu.make_async_remote_copy(
            src_ref=src, dst_ref=dst, send_sem=send.at[k], recv_sem=recv.at[k],
            device_id={"ent": to(k)}, device_id_type=MESH,
        )

    def rel_copy(j, slot):
        return pltpu.make_async_remote_copy(
            src_ref=relations, dst_ref=rels.at[slot], send_sem=sr.at[j], recv_sem=rr.at[j],
            device_id={"rep": lax.rem(mine + j, m)}, device_id_type=MESH,
        )

    def each(body):
        lax.fori_loop(1, n, lambda k, c: (body(k), c)[1], 0)

    barrier = pltpu.get_barrier_semaphore()
    each(lambda k: pl.semaphore_signal(barrier, inc=1, device_id={"ent": to(k)}, device_id_type=MESH))
    for j in range(1, m):
        pl.semaphore_signal(barrier, inc=1, device_id={"rep": lax.rem(mine + j, m)}, device_id_type=MESH)

    def gather(d):
        def one(i, c):
            row = d * chunk + i
            off = anchor[row] - start
            inside = jnp.logical_and(off >= 0, off < ents)
            value = table[pl.ds(jnp.clip(off, 0, ents - 1), 1), :]
            asend[pl.ds(row, 1), :] = jnp.where(inside, value, 0.0)
            return c
        lax.fori_loop(0, chunk, one, 0, unroll=8)

    pl.semaphore_wait(barrier, n - 1 + m - 1)
    for j in range(1, m):
        rel_copy(j, mine).start()

    def a_copy(k):
        return ent_copy(asend.at[at(to(k))], arecv.at[k], sa, ra, k)

    def a_step(k):
        gather(to(k))
        a_copy(k).start()

    each(a_step)
    gather(me)
    rels[mine] = relations[...]

    def split(i, c):
        part = pl.ds(pl.multiple_of(i * 256, 256), 256)
        t_hi[part, :], t_lo[part, :] = halves(table[part, :])
        return c
    lax.fori_loop(0, ents // 256, split, 0)

    for j in range(1, m):
        rel_copy(j, lax.rem(mine - j + m, m)).wait_recv()

    def pick(i, c):
        first, second = rel_one[me * chunk + i], rel_two[me * chunk + i]
        r1[pl.ds(i, 1), :] = rels[first // nrel, pl.ds(lax.rem(first, nrel), 1), :]
        r2[pl.ds(i, 1), :] = rels[second // nrel, pl.ds(lax.rem(second, nrel), 1), :]
        return c
    lax.fori_loop(0, chunk, pick, 0, unroll=8)

    acc[...] = asend[at(me), :]

    def a_sum(k):
        a_copy(k).wait_recv()
        acc[...] += arecv[k]
    each(a_sum)
    q1[at(me), :] = cmul(acc[...], r1[...])

    def share(q, send, recv):
        each(lambda k: ent_copy(q.at[at(me)], q.at[at(me)], send, recv, k).start())

    def arrived(q, send, recv):
        each(lambda k: ent_copy(q.at[at(me)], q.at[at(source(k))], send, recv, k).wait_recv())

    share(q1, sb, rb)
    arrived(q1, sb, rb)

    def score(q, b):
        part = slice(b * block, (b + 1) * block)
        query = halves(q[part, :])
        peak = None
        for t in range(ents // tile):
            cols = slice(t * tile, (t + 1) * tile)
            s = dot3(query, (t_hi[cols, :], t_lo[cols, :]), NT)
            scores[part, cols] = s
            top = jnp.max(s, axis=1, keepdims=True)
            peak = top if peak is None else jnp.maximum(peak, top)
        return part, peak

    def c_copy(k):
        return ent_copy(csend.at[at(to(k))], crecv.at[k], sc, rc, k)

    for b in range(rows // block):
        part, peak = score(q1, b)
        total = jnp.zeros((block, 1), F32)
        summed = jnp.zeros((block, width), F32)
        for t in range(ents // tile):
            cols = slice(t * tile, (t + 1) * tile)
            w = jnp.exp(scores[part, cols] - peak)
            total += jnp.sum(w, axis=1, keepdims=True)
            summed += dot3(halves(w), (t_hi[cols, :], t_lo[cols, :]), NN)
        csend[part, :width] = summed
        lane = lax.broadcasted_iota(jnp.int32, (block, 128), 1)
        csend[part, width:] = jnp.where(lane < 64, peak, total)
    each(lambda k: c_copy(k).start())

    crecv[0] = csend[at(me), :]
    each(lambda k: c_copy(k).wait_recv())
    peak = lax.fori_loop(
        1, n, lambda k, p: jnp.maximum(p, crecv[k, :, width : width + 1]), crecv[0, :, width : width + 1]
    )
    acc[...] = jnp.zeros_like(acc)

    def c_sum(k, total):
        scale = jnp.exp(crecv[k, :, width : width + 1] - peak)
        acc[...] += crecv[k, :, :width] * scale
        return total + crecv[k, :, width + 127 : width + 128] * scale
    total = lax.fori_loop(0, n, c_sum, jnp.zeros((chunk, 1), F32))
    q2[at(me), :] = cmul(acc[...] / total, r2[...])
    share(q2, sd, rd)
    arrived(q2, sd, rd)

    def out_copy(b):
        part = pl.ds(b * block, block)
        return pltpu.make_async_copy(scores.at[part], scores_out.at[part], so.at[b])

    for b in range(rows // block):
        part, peak = score(q2, b)
        out_copy(b).start()
        mass = jnp.zeros((block, 1), F32)
        for t in range(ents // tile):
            cols = slice(t * tile, (t + 1) * tile)
            mass += jnp.sum(jnp.exp(scores[part, cols] - peak), axis=1, keepdims=True)
        lse = jnp.broadcast_to(peak + jnp.log(mass), (block, 128))
        esend[:, part] = lse.T[:8, :]

    def e_copy(k):
        return ent_copy(esend, erecv.at[k], se, re, k)
    each(lambda k: e_copy(k).start())
    erecv[0] = esend[...]
    each(lambda k: e_copy(k).wait_recv())
    top = lax.fori_loop(1, n, lambda k, p: jnp.maximum(p, erecv[k]), erecv[0])
    mass = lax.fori_loop(0, n, lambda k, c: c + jnp.exp(erecv[k] - top), jnp.zeros_like(top))
    lse_out[...] = top + jnp.log(mass)

    for j in range(1, m):
        rel_copy(j, mine).wait_send()

    def drain(k):
        a_copy(k).wait_send()
        ent_copy(q1.at[at(me)], q1.at[at(me)], sb, rb, k).wait_send()
        c_copy(k).wait_send()
        ent_copy(q2.at[at(me)], q2.at[at(me)], sd, rd, k).wait_send()
        e_copy(k).wait_send()
    each(drain)
    for b in range(rows // block):
        out_copy(b).wait()


def solution(mesh):
    n, m = mesh.shape["ent"], mesh.shape["rep"]

    def on_device(table, relations, anchor, rel_one, rel_two):
        ents, width = table.shape
        rows = anchor.shape[0]
        chunk = rows // n
        block = min(rows, 256)
        tile = min(ents, 512)
        vmem, smem = pl.BlockSpec(memory_space=pltpu.VMEM), pl.BlockSpec(memory_space=pltpu.SMEM)
        dma = pltpu.SemaphoreType.DMA
        scores, lse = pl.pallas_call(
            functools.partial(kernel, n, m, tile, block),
            out_shape=(
                jax.ShapeDtypeStruct((rows, ents), F32),
                jax.ShapeDtypeStruct((8, rows), F32),
            ),
            in_specs=[vmem, vmem, smem, smem, smem],
            out_specs=(pl.BlockSpec(memory_space=pl.ANY), vmem),
            scratch_shapes=[
                pltpu.VMEM((ents, width), BF16),
                pltpu.VMEM((ents, width), BF16),
                pltpu.VMEM((rows, ents), F32),
                pltpu.VMEM((rows, width), F32),
                pltpu.VMEM((n, chunk, width), F32),
                pltpu.VMEM((m, relations.shape[0], width), F32),
                pltpu.VMEM((chunk, width), F32),
                pltpu.VMEM((chunk, width), F32),
                pltpu.VMEM((chunk, width), F32),
                pltpu.VMEM((rows, width), F32),
                pltpu.VMEM((rows, width), F32),
                pltpu.VMEM((rows, width + 128), F32),
                pltpu.VMEM((n, chunk, width + 128), F32),
                pltpu.VMEM((n, 8, rows), F32),
                pltpu.VMEM((8, rows), F32),
                dma((n,)), dma((n,)), dma((m,)), dma((m,)),
                dma((n,)), dma((n,)), dma((n,)), dma((n,)),
                dma((n,)), dma((n,)), dma((n,)), dma((n,)),
                dma((rows // block,)),
            ],
            compiler_params=pltpu.CompilerParams(
                collective_id=0, has_side_effects=True, vmem_limit_bytes=52 * 1024 * 1024
            ),
            cost_estimate=pl.CostEstimate(
                flops=18 * rows * ents * width, bytes_accessed=4 * rows * ents,
                transcendentals=2 * rows * ents,
            ),
        )(table, relations, anchor, rel_one, rel_two)
        return scores - lse[0][:, None]

    return jax.shard_map(
        on_device,
        mesh=mesh,
        in_specs=(P("ent", None), P("rep", None), P("rep"), P("rep"), P("rep")),
        out_specs=P("rep", "ent"),
        check_vma=False,
    )
```

time: 269 us -> 99.8 us (0.37)
  waiting for transfers between devices: 107 us -> 0 us
  Pallas kernels: 0 us -> 88.4 us
  blocking collectives: 84.4 us -> 0 us
  matrix products: 33 us -> 0 us
  other arithmetic: 24.3 us -> 8.14 us
  between operations: 13.5 us -> 0.02 us
  local copies, waits for them, and re-layouts: 7.02 us -> 2.98 us
    psum x2 -> x0, waiting for transfers between devices: 107 us -> none  [the longest x1 59 us: on_device(): anchor_emb = lax.psum(local_rows * inside[:, None], 'ent')]
    pallas_call x0 -> x1, Pallas kernels: none -> 88.4 us  [on_device(): pl.pallas_call(functools.partial(kernel, n, m, tile, block), out_shape=(j...]
    pmax x2 -> x0, blocking collectives: 39.4 us -> none  [the longest x1 19.7 us: on_device(): peak = lax.pmax(local_peak, 'ent')]
    psum x2 -> x0, blocking collectives: 34.5 us -> none  [the longest x1 17.3 us: on_device(): lax.psum((jnp.sum(weights, axis=1), weighted(weights, table)), 'ent')]
    dot_general x3 -> x0, matrix products: 33 us -> none  [the longest x2 21.8 us: against(): lax.dot_general(query, table, (((1,), (1,)), ((), ())), precision=lax.Pre...]
    all_gather x1 -> x0, blocking collectives: 10.6 us -> none  [on_device(): rel_all = lax.all_gather(relations, 'rep', axis=0, tiled=True)]
    reduce_sum x2 -> x0, other arithmetic: 9.38 us -> none  [the longest x1 4.75 us: on_device(): jnp.sum(weights, axis=1)]
    gather x3 -> x0, local copies, waits for them, and re-layouts: 6.91 us -> none  [the longest x1 3.76 us: on_device(): local_rows = jnp.take(table, jnp.clip(offset, 0, rows - 1), axis=0)]
  transfers between devices with their start and end apart: 2 -> 0, of which waited for: 2 -> 0; matrix products, arithmetic and copies ran while one was open for 4% -> 0% of each run, Pallas kernels for 0% -> 0%
where the time goes in v1:
time: 99.8 us; the launch traced here: 99.5 us
  Pallas kernels  88.4 us (89%)
  other arithmetic  8.14 us (8%)
  local copies, waits for them, and re-layouts  2.98 us (3%)
    pallas_call x1, Pallas kernels, on_device(): pl.pallas_call(functools.partial(kernel, n, m, tile, block), out_shape=(j...  88.4 us
    sub x1, other arithmetic, on_device(): return scores - lse[0][:, None]  8.14 us
    unnamed x8, local copies, waits for them, and re-layouts  2.98 us

profile of v1, /device:TPU:0, one launch (start us, length us, event | category | flops | bytes accessed | tf_op | source)
XLA Modules:
  0.0 99.5 jit_solution(3371415637283415436)
XLA Ops:
  0.0 0.0 copy-start
  0.0 0.9 copy-done
  0.9 0.0 copy-start.1
  0.9 0.7 copy-done.1
  1.6 0.0 copy-start.2
  1.6 0.7 copy-done.2
  2.3 0.0 copy-start.3
  2.3 0.7 copy-done.3
  3.0 88.4 %shard_map.55 = (f32[512,4096]{1,0:T(8,128)}, f32[8,512]{1,0:T(8,128)S(1)}) custom-call(f32[4096,256]{1,0:T(8,128)} %table.1, f32[206,256]{1,0:T(8,128)S(1)} %copy-done, s32[512]{0:T(512)S(1)} %copy-done.1, s32[512]{0:T(512)S(1)} %copy-done.2, s32[512]{0:T(512)S(1)} %copy-done.3), custom_call_target="tpu_custom_call" | custom-call | flops 9663676416 | bytes 8388608 | tf_op jit(solution)/shard_map/pallas_call | solution.py:232
  91.4 8.1 %broadcast_subtract_fusion = f32[512,4096]{1,0:T(8,128)} fusion(f32[512,4096]{1,0:T(8,128)} %get-tuple-element.7, f32[512]{0:T(512)S(1)} %bitcast.1), kind=kLoop, calls=%fused_computation | loop fusion | flops 2097152 | bytes 16779264 | tf_op jit(solution)/shard_map/sub | solution.py:269
  (1 shorter events, 0.0 us)
Async XLA Ops:
  0.0 0.9 copy-start
  0.9 0.7 copy-start.1
  1.6 0.7 copy-start.2
  2.3 0.7 copy-start.3

commit v2 on v1

--- a/solution.py
+++ b/solution.py
@@ -73,6 +73,23 @@
     def each(body):
         lax.fori_loop(1, n, lambda k, c: (body(k), c)[1], 0)
 
+    per = block // chunk
+    blocks = rows // block
+    near = me // per
+
+    def among(first, count, body):
+        def one(i, c):
+            k = lax.rem(lax.rem(first + i, n) - me + n, n)
+
+            @pl.when(k != 0)
+            def _():
+                body(k)
+            return c
+        lax.fori_loop(0, count, one, 0)
+
+    def far_first(body):
+        among((near + 1) * per, n, body)
+
     barrier = pltpu.get_barrier_semaphore()
     each(lambda k: pl.semaphore_signal(barrier, inc=1, device_id={"ent": to(k)}, device_id_type=MESH))
     for j in range(1, m):
@@ -99,7 +116,7 @@
         gather(to(k))
         a_copy(k).start()
 
-    each(a_step)
+    far_first(a_step)
     gather(me)
     rels[mine] = relations[...]
 
@@ -128,16 +145,26 @@
     q1[at(me), :] = cmul(acc[...], r1[...])
 
     def share(q, send, recv):
-        each(lambda k: ent_copy(q.at[at(me)], q.at[at(me)], send, recv, k).start())
-
-    def arrived(q, send, recv):
-        each(lambda k: ent_copy(q.at[at(me)], q.at[at(source(k))], send, recv, k).wait_recv())
+        far_first(lambda k: ent_copy(q.at[at(me)], q.at[at(me)], send, recv, k).start())
+
+    def arrived(q, send, recv, b):
+        def one(i, c):
+            s = b * per + i
+            k = lax.rem(me - s + n, n)
+
+            @pl.when(k != 0)
+            def _():
+                ent_copy(q.at[at(me)], q.at[at(s)], send, recv, k).wait_recv()
+            return c
+        lax.fori_loop(0, per, one, 0)
+
+    def place(step):
+        return lax.rem(near + step, blocks)
 
     share(q1, sb, rb)
-    arrived(q1, sb, rb)
 
     def score(q, b):
-        part = slice(b * block, (b + 1) * block)
+        part = pl.ds(pl.multiple_of(b * block, block), block)
         query = halves(q[part, :])
         peak = None
         for t in range(ents // tile):
@@ -151,7 +178,9 @@
     def c_copy(k):
         return ent_copy(csend.at[at(to(k))], crecv.at[k], sc, rc, k)
 
-    for b in range(rows // block):
+    for step in range(blocks):
+        b = place(step)
+        arrived(q1, sb, rb, b)
         part, peak = score(q1, b)
         total = jnp.zeros((block, 1), F32)
         summed = jnp.zeros((block, width), F32)
@@ -163,7 +192,7 @@
         csend[part, :width] = summed
         lane = lax.broadcasted_iota(jnp.int32, (block, 128), 1)
         csend[part, width:] = jnp.where(lane < 64, peak, total)
-    each(lambda k: c_copy(k).start())
+        among(b * per, per, lambda k: c_copy(k).start())
 
     crecv[0] = csend[at(me), :]
     each(lambda k: c_copy(k).wait_recv())
@@ -179,13 +208,14 @@
     total = lax.fori_loop(0, n, c_sum, jnp.zeros((chunk, 1), F32))
     q2[at(me), :] = cmul(acc[...] / total, r2[...])
     share(q2, sd, rd)
-    arrived(q2, sd, rd)
 
     def out_copy(b):
-        part = pl.ds(b * block, block)
+        part = pl.ds(pl.multiple_of(b * block, block), block)
         return pltpu.make_async_copy(scores.at[part], scores_out.at[part], so.at[b])
 
-    for b in range(rows // block):
+    for step in range(blocks):
+        b = place(step)
+        arrived(q2, sd, rd, b)
         part, peak = score(q2, b)
         out_copy(b).start()
         mass = jnp.zeros((block, 1), F32)
@@ -259,7 +289,7 @@
                 dma((rows // block,)),
             ],
             compiler_params=pltpu.CompilerParams(
-                collective_id=0, has_side_effects=True, vmem_limit_bytes=52 * 1024 * 1024
+                collective_id=0, has_side_effects=True, vmem_limit_bytes=32 * 1024 * 1024
             ),
             cost_estimate=pl.CostEstimate(
                 flops=18 * rows * ents * width, bytes_accessed=4 * rows * ents,

time: 99.8 us -> 99.4 us (level)
  other arithmetic: 8.14 us -> 4.4 us
  local copies, waits for them, and re-layouts: 2.98 us -> 5.17 us
  Pallas kernels: 88.4 us -> 89.6 us
    sub x1, other arithmetic: 8.14 us -> 4.4 us  [on_device(): return scores - lse[0][:, None]]
    unnamed x8 -> x10, local copies, waits for them, and re-layouts: 2.98 us -> 5.16 us
    pallas_call x1, Pallas kernels: 88.4 us -> 89.6 us  [on_device(): pl.pallas_call(functools.partial(kernel, n, m, tile, block), out_shape=(j...]
where the time goes in v2:
time: 99.4 us; the launch traced here: 99.2 us
  Pallas kernels  89.6 us (90%)
  local copies, waits for them, and re-layouts  5.17 us (5%)
  other arithmetic  4.4 us (4%)
    pallas_call x1, Pallas kernels, on_device(): pl.pallas_call(functools.partial(kernel, n, m, tile, block), out_shape=(j...  89.6 us
    unnamed x10, local copies, waits for them, and re-layouts  5.16 us
    sub x1, other arithmetic, on_device(): return scores - lse[0][:, None]  4.4 us

profile of v2, /device:TPU:0, one launch (start us, length us, event | category | flops | bytes accessed | tf_op | source)
XLA Modules:
  0.0 99.2 jit_solution(12217262338482090274)
XLA Ops:
  0.0 0.0 copy-start
  0.0 2.2 %copy-done = f32[4096,256]{1,0:T(8,128)S(1)} copy-done((f32[4096,256]{1,0:T(8,128)S(1)}, f32[4096,256]{1,0:T(8,128)}, u32[]{:S(2)}) %copy-start) | copy-done | bytes 4194328
  2.2 0.0 copy-start.1
  2.2 0.9 copy-done.1
  3.1 0.0 copy-start.2
  3.1 0.7 copy-done.2
  3.8 0.0 copy-start.3
  3.8 0.7 copy-done.3
  4.5 0.0 copy-start.4
  4.5 0.7 copy-done.4
  5.2 89.6 %shard_map.55 = (f32[512,4096]{1,0:T(8,128)S(1)}, f32[8,512]{1,0:T(8,128)S(1)}) custom-call(f32[4096,256]{1,0:T(8,128)S(1)} %copy-done, f32[206,256]{1,0:T(8,128)S(1)} %copy-done.1, s32[512]{0:T(512)S(1)} %copy-done.2, s32[512]{0:T(512)S(1)} %copy-done.3, s32[512]{0:T(512)S(1)} %copy-done.4), custom_call_target="tpu_custom_call" | custom-call | flops 9663676416 | bytes 8388608 | tf_op jit(solution)/shard_map/pallas_call | solution.py:262
  94.8 4.4 %broadcast_subtract_fusion = f32[512,4096]{1,0:T(8,128)} fusion(f32[512,4096]{1,0:T(8,128)S(1)} %get-tuple-element.7, f32[512]{0:T(512)S(1)} %bitcast.1), kind=kLoop, calls=%fused_computation | loop fusion | flops 2097152 | bytes 16779264 | tf_op jit(solution)/shard_map/sub | solution.py:299
  (1 shorter events, 0.0 us)
Async XLA Ops:
  0.0 2.2 %copy-start = (f32[4096,256]{1,0:T(8,128)S(1)}, f32[4096,256]{1,0:T(8,128)}, u32[]{:S(2)}) copy-start(f32[4096,256]{1,0:T(8,128)} %table.1) | copy-start | bytes 12582916
  2.2 0.9 copy-start.1
  3.1 0.7 copy-start.2
  3.8 0.7 copy-start.3
  4.5 0.7 copy-start.4

commit v3 on v2

--- a/solution.py
+++ b/solution.py
@@ -255,7 +255,7 @@
         ents, width = table.shape
         rows = anchor.shape[0]
         chunk = rows // n
-        block = min(rows, 256)
+        block = min(rows, 512)
         tile = min(ents, 512)
         vmem, smem = pl.BlockSpec(memory_space=pltpu.VMEM), pl.BlockSpec(memory_space=pltpu.SMEM)
         dma = pltpu.SemaphoreType.DMA

time: 99.4 us -> 97.4 us (0.980)
  Pallas kernels: 89.6 us -> 87.6 us
    pallas_call x1, Pallas kernels: 89.6 us -> 87.6 us  [on_device(): pl.pallas_call(functools.partial(kernel, n, m, tile, block), out_shape=(j...]
where the time goes in v3:
time: 97.4 us; the launch traced here: 97.2 us
  Pallas kernels  87.6 us (90%)
  local copies, waits for them, and re-layouts  5.17 us (5%)
  other arithmetic  4.4 us (5%)
    pallas_call x1, Pallas kernels, on_device(): pl.pallas_call(functools.partial(kernel, n, m, tile, block), out_shape=(j...  87.6 us
    unnamed x10, local copies, waits for them, and re-layouts  5.16 us
    sub x1, other arithmetic, on_device(): return scores - lse[0][:, None]  4.4 us

profile of v3, /device:TPU:0, one launch (start us, length us, event | category | flops | bytes accessed | tf_op | source)
XLA Modules:
  0.0 97.2 jit_solution(11846916194116848505)
XLA Ops:
  0.0 0.0 copy-start
  0.0 2.2 %copy-done = f32[4096,256]{1,0:T(8,128)S(1)} copy-done((f32[4096,256]{1,0:T(8,128)S(1)}, f32[4096,256]{1,0:T(8,128)}, u32[]{:S(2)}) %copy-start) | copy-done | bytes 4194328
  2.2 0.0 copy-start.1
  2.2 0.9 copy-done.1
  3.1 0.0 copy-start.2
  3.1 0.7 copy-done.2
  3.8 0.0 copy-start.3
  3.8 0.7 copy-done.3
  4.5 0.0 copy-start.4
  4.5 0.7 copy-done.4
  5.2 87.6 %shard_map.55 = (f32[512,4096]{1,0:T(8,128)S(1)}, f32[8,512]{1,0:T(8,128)S(1)}) custom-call(f32[4096,256]{1,0:T(8,128)S(1)} %copy-done, f32[206,256]{1,0:T(8,128)S(1)} %copy-done.1, s32[512]{0:T(512)S(1)} %copy-done.2, s32[512]{0:T(512)S(1)} %copy-done.3, s32[512]{0:T(512)S(1)} %copy-done.4), custom_call_target="tpu_custom_call" | custom-call | flops 9663676416 | bytes 8388608 | tf_op jit(solution)/shard_map/pallas_call | solution.py:262
  92.8 4.4 %broadcast_subtract_fusion = f32[512,4096]{1,0:T(8,128)} fusion(f32[512,4096]{1,0:T(8,128)S(1)} %get-tuple-element.7, f32[512]{0:T(512)S(1)} %bitcast.1), kind=kLoop, calls=%fused_computation | loop fusion | flops 2097152 | bytes 16779264 | tf_op jit(solution)/shard_map/sub | solution.py:299
  (1 shorter events, 0.0 us)
Async XLA Ops:
  0.0 2.2 %copy-start = (f32[4096,256]{1,0:T(8,128)S(1)}, f32[4096,256]{1,0:T(8,128)}, u32[]{:S(2)}) copy-start(f32[4096,256]{1,0:T(8,128)} %table.1) | copy-start | bytes 12582916
  2.2 0.9 copy-start.1
  3.1 0.7 copy-start.2
  3.8 0.7 copy-start.3
  4.5 0.7 copy-start.4

commit v4 on v3

--- a/solution.py
+++ b/solution.py
@@ -28,7 +28,9 @@
 
 
 def dot3(a, b, contract):
-    return dot(a[0], b[0], contract) + (dot(a[0], b[1], contract) + dot(a[1], b[0], contract))
+    left = jnp.concatenate([a[0], a[0], a[1]], axis=contract[0][0])
+    right = jnp.concatenate([b[0], b[1], b[0]], axis=contract[1][0])
+    return dot(left, right, contract)
 
 
 NT = ((1,), (1,))

time: 97.4 us -> 97.6 us (level)
  no operation moved by 1% of the time
where the time goes in v4:
time: 97.6 us; the launch traced here: 97.3 us
  Pallas kernels  87.7 us (90%)
  local copies, waits for them, and re-layouts  5.17 us (5%)
  other arithmetic  4.4 us (5%)
    pallas_call x1, Pallas kernels, on_device(): pl.pallas_call(functools.partial(kernel, n, m, tile, block), out_shape=(j...  87.7 us
    unnamed x10, local copies, waits for them, and re-layouts  5.16 us
    sub x1, other arithmetic, on_device(): return scores - lse[0][:, None]  4.4 us

profile of v4, /device:TPU:0, one launch (start us, length us, event | category | flops | bytes accessed | tf_op | source)
XLA Modules:
  0.0 97.3 jit_solution(7755154554236542981)
XLA Ops:
  0.0 0.0 copy-start
  0.0 2.2 %copy-done = f32[4096,256]{1,0:T(8,128)S(1)} copy-done((f32[4096,256]{1,0:T(8,128)S(1)}, f32[4096,256]{1,0:T(8,128)}, u32[]{:S(2)}) %copy-start) | copy-done | bytes 4194328
  2.2 0.0 copy-start.1
  2.2 0.9 copy-done.1
  3.1 0.0 copy-start.2
  3.1 0.7 copy-done.2
  3.8 0.0 copy-start.3
  3.8 0.7 copy-done.3
  4.5 0.0 copy-start.4
  4.5 0.7 copy-done.4
  5.2 87.7 %shard_map.55 = (f32[512,4096]{1,0:T(8,128)S(1)}, f32[8,512]{1,0:T(8,128)S(1)}) custom-call(f32[4096,256]{1,0:T(8,128)S(1)} %copy-done, f32[206,256]{1,0:T(8,128)S(1)} %copy-done.1, s32[512]{0:T(512)S(1)} %copy-done.2, s32[512]{0:T(512)S(1)} %copy-done.3, s32[512]{0:T(512)S(1)} %copy-done.4), custom_call_target="tpu_custom_call" | custom-call | flops 9663676416 | bytes 8388608 | tf_op jit(solution)/shard_map/pallas_call | solution.py:264
  92.9 4.4 %broadcast_subtract_fusion = f32[512,4096]{1,0:T(8,128)} fusion(f32[512,4096]{1,0:T(8,128)S(1)} %get-tuple-element.7, f32[512]{0:T(512)S(1)} %bitcast.1), kind=kLoop, calls=%fused_computation | loop fusion | flops 2097152 | bytes 16779264 | tf_op jit(solution)/shard_map/sub | solution.py:301
  (1 shorter events, 0.0 us)
Async XLA Ops:
  0.0 2.2 %copy-start = (f32[4096,256]{1,0:T(8,128)S(1)}, f32[4096,256]{1,0:T(8,128)}, u32[]{:S(2)}) copy-start(f32[4096,256]{1,0:T(8,128)} %table.1) | copy-start | bytes 12582916
  2.2 0.9 copy-start.1
  3.1 0.7 copy-start.2
  3.8 0.7 copy-start.3
  4.5 0.7 copy-start.4
